TPU v7x, 1024 devices: a whole 4x8x16 slice. The times are simulated.
1024 devices in a mesh: seq: 128 (over y, z), head: 8 (over x, core).
Axes of the slice: x: 4, y: 8, z: 16, core: 2. Of those that a mesh axis runs over, the one named last changes fastest.
Arguments:
- queries: float32 [16384, 2048], P('seq', 'head'), may hold values from -6 to 6
- keys: float32 [16384, 2048], P('seq', 'head'), may hold values from -0.53033006 to 0.53033006
- values: float32 [16384, 2048], P('seq', 'head'), may hold values from -6 to 6
- out_grad: bfloat16 [16384, 2048], P('seq', 'head'), may hold values from -6 to 6
- w_out: bfloat16 [2048, 2048], P('head'), may hold values from -0.125 to 0.125
- ridge: float32 [16], P('head'), may hold values from 0.25 to 4
Outputs:
- grad_queries: float32 [16384, 2048], P('seq', 'head')
- grad_keys: float32 [16384, 2048], P('seq', 'head')
- grad_values: float32 [16384, 2048], P('seq', 'head')
All inputs are finite; a program needn't handle non-finite values.
Results may differ from a plain program's by a relative error of at most 0.00035.
Values may be sent and summed in bfloat16 or wider, within the bound.
No kernel may reach another device: no remote copies, remote signals or barrier semaphores. Data moves between devices by JAX's collectives and lax.ppermute only.
A program may use at most 128 MiB of HBM per device.

v0:
```python
import jax
import jax.numpy as jnp
from jax import lax
from jax.sharding import PartitionSpec as P

ITERS = 2


highest = lax.Precision.HIGHEST


def carried_in(value, axis, join, neutral, backward):
    count, mine = (lax.axis_size(axis), lax.axis_index(axis))
    pieces = jax.tree.map(lambda part: lax.all_gather(part, axis), value)
    if backward:
        pieces = jax.tree.map(lambda part: part[::-1], pieces)
        mine = count - 1 - mine
    total = jax.tree.map(
        lambda part, zero: jnp.full_like(part, 0) + jnp.asarray(zero, part.dtype), value, neutral
    )

    def hop(position, total):
        longer = join(total, jax.tree.map(lambda part: part[position], pieces))
        return jax.tree.map(lambda new, old: jnp.where(position < mine, new, old), longer, total)

    return lax.fori_loop(0, count - 1, hop, total)


def lower_mask(count):
    rows = lax.broadcasted_iota(jnp.int32, (count, count), 0)
    cols = lax.broadcasted_iota(jnp.int32, (count, count), 1)
    return (rows >= cols).astype(jnp.float32)


def local_out(query_heads, key_heads, value_heads, cov_before, valkey_before, ridge_heads):
    mask = lower_mask(query_heads.shape[1])
    solution = jnp.zeros_like(query_heads)
    resid = query_heads
    direction = query_heads
    norm_now = jnp.sum(resid * resid, axis=-1, keepdims=True)
    for step in range(ITERS):
        apply_carried = jnp.einsum("hij,htj->hti", cov_before, direction, precision=highest)
        apply_scores = jnp.einsum("htd,hsd->hts", direction, key_heads, precision=highest) * mask
        inner = jnp.einsum("hts,hsd->htd", apply_scores, key_heads, precision=highest)
        image = apply_carried + inner + ridge_heads[:, None, None] * direction
        alpha = norm_now / (jnp.sum(direction * image, axis=-1, keepdims=True) + 1e-06)
        solution = solution + alpha * direction
        resid = resid - alpha * image
        norm_next = jnp.sum(resid * resid, axis=-1, keepdims=True)
        direction = resid + norm_next / (norm_now + 1e-06) * direction
        norm_now = norm_next
    carried = jnp.einsum("hij,htj->hti", valkey_before, solution, precision=highest)
    scores = jnp.einsum("htd,hsd->hts", solution, key_heads, precision=highest) * mask
    return carried + jnp.einsum("hts,hsd->htd", scores, value_heads, precision=highest)


def state_sums(key_heads, value_heads):
    cov_sums = jnp.einsum("htd,hte->hde", key_heads, key_heads, precision=highest)
    valkey_sums = jnp.einsum("hti,htj->hij", value_heads, key_heads, precision=highest)
    return (cov_sums, valkey_sums)


def add_pair(earlier, later):
    return (earlier[0] + later[0], earlier[1] + later[1])


def on_device(queries, keys, values, out_grad, w_out, ridge):
    tok_rows = queries.shape[0]
    group_heads = ridge.shape[0]
    head_size = queries.shape[1] // group_heads
    d_out = lax.dot_general(
        lax.all_gather(out_grad, "head", axis=1, tiled=True),
        w_out,
        (((1,), (1,)), ((), ())),
        preferred_element_type=jnp.float32,
    )

    def split_heads(array):
        return array.reshape(tok_rows, group_heads, head_size).transpose(1, 0, 2)

    query_heads = split_heads(queries)
    key_heads = split_heads(keys)
    value_heads = split_heads(values)
    grad_heads = split_heads(d_out)
    cov_sums, valkey_sums = state_sums(key_heads, value_heads)
    zeros_state = jnp.zeros((group_heads, head_size, head_size), jnp.float32)
    cov_before, valkey_before = carried_in(
        (cov_sums, valkey_sums), "seq", add_pair, (zeros_state, zeros_state), False
    )

    def forward(query_in, key_in, value_in, cov_in, valkey_in):
        return local_out(query_in, key_in, value_in, cov_in, valkey_in, ridge)

    unused, pull = jax.vjp(forward, query_heads, key_heads, value_heads, cov_before, valkey_before)
    grad_query, grad_key_local, grad_value_local, grad_cov, grad_valkey = pull(grad_heads)
    later_cov, later_valkey = carried_in(
        (grad_cov, grad_valkey), "seq", add_pair, (zeros_state, zeros_state), True
    )
    unused_sums, pull_sums = jax.vjp(state_sums, key_heads, value_heads)
    grad_key_state, grad_value_state = pull_sums((later_cov, later_valkey))

    def join_heads(array):
        return array.transpose(1, 0, 2).reshape(tok_rows, group_heads * head_size)

    return (
        join_heads(grad_query),
        join_heads(grad_key_local + grad_key_state),
        join_heads(grad_value_local + grad_value_state),
    )


def solution(mesh):
    in_specs = (
        P("seq", "head"),
        P("seq", "head"),
        P("seq", "head"),
        P("seq", "head"),
        P("head", None),
        P("head"),
    )
    out_specs = (P("seq", "head"), P("seq", "head"), P("seq", "head"))
    return jax.shard_map(
        on_device, mesh=mesh, in_specs=in_specs, out_specs=out_specs, check_vma=False
    )
```

profile of v0, /device:TPU:1, one launch (start us, length us, event | category | flops | bytes accessed | tf_op | source)
XLA Modules:
  0.0 1075.1 jit_solution(17741079917296407340)
XLA Ops:
  7.3 2.1 fusion.19
  9.4 2.0 fusion.23
  12.6 27.3 %all_gather.31 = bf16[128,2048]{1,0:T(8,128)(2,1)S(1)} all-gather(bf16[128,256]{1,0:T(8,128)(2,1)} %param.13), channel_id=1, replica_groups=mesh['seq'=128,'head'=8] {'head'}, dimensions={1}, use_global_device_ids=true | all-gather | bytes 589824 | tf_op jit(solution)/shard_map/all_gather | solution.py:72
  39.9 1.3 convolution_multiply_fusion.5
  41.2 1.3 fusion.22
  42.9 1.3 convolution_multiply_fusion.3
  44.2 1.3 fusion.21
  45.5 164.0 %all-gather.11.cloned.1.call-done = f32[256,128,128]{2,1,0:T(8,128)} async-done(((f32[2,128,128]{2,1,0:T(8,128)}), f32[256,128,128]{2,1,0:T(8,128)}) %all-gather.11.cloned.1.call-update) | async-done | bytes 16777232 | tf_op jit(solution)/shard_map/all_gather | solution.py:14
  209.5 187.6 %all-gather.9.cloned.1.call-done = f32[256,128,128]{2,1,0:T(8,128)} async-done(((f32[2,128,128]{2,1,0:T(8,128)}), f32[256,128,128]{2,1,0:T(8,128)}) %all-gather.9.cloned.1.call-update) | async-done | bytes 16777232 | tf_op jit(solution)/shard_map/all_gather | solution.py:14
  397.1 138.1 %while.32 = (s32[]{:T(128)}, f32[2,128,128]{2,1,0:T(8,128)S(1)}, f32[2,128,128]{2,1,0:T(8,128)S(1)}, s32[]{:T(128)}, f32[128,2,128,128]{3,2,1,0:T(8,128)}, /*ind...) while((s32[]{:T(128)}, f32[2,128,128]{2,1,0:T(8,128)S(1)}, f32[2,128,128]{2,1,0:T(8,128)S(1)}, ...), condition=%wide.region_2.3_spmd.clone, body=%wide.region_1.2_spmd.clone.sunk | while | flops 196612 | bytes 786549 | solution.py:26
  398.2 1.1 add_select_fusion.6
  400.3 1.1 add_select_fusion.6
  402.5 1.1 add_select_fusion.6
  405.8 1.1 add_select_fusion.6
  407.9 1.1 add_select_fusion.6
  410.1 1.1 add_select_fusion.6
  411.2 1.1 add_select_fusion.6
  413.4 1.1 add_select_fusion.6
  415.6 1.1 add_select_fusion.6
  417.7 1.1 add_select_fusion.6
  418.8 1.1 add_select_fusion.6
  421.0 1.1 add_select_fusion.6
  423.2 1.1 add_select_fusion.6
  426.4 1.1 add_select_fusion.6
  428.6 1.1 add_select_fusion.6
  430.8 1.1 add_select_fusion.6
  431.9 1.1 add_select_fusion.6
  434.0 1.1 add_select_fusion.6
  436.2 1.1 add_select_fusion.6
  438.4 1.1 add_select_fusion.6
  439.5 1.1 add_select_fusion.6
  441.7 1.1 add_select_fusion.6
  443.8 1.1 add_select_fusion.6
  447.1 1.1 add_select_fusion.6
  449.3 1.1 add_select_fusion.6
  451.4 1.1 add_select_fusion.6
  452.5 1.1 add_select_fusion.6
  454.7 1.1 add_select_fusion.6
  535.4 1.1 multiply_reduce_fusion
  536.6 1.3 convolution_multiply_fusion.4
  538.2 1.3 multiply_reduce_fusion.4
  539.5 1.3 convolution_multiply_fusion.2
  541.2 1.3 fusion.20
  549.8 178.1 %all-gather.13.cloned.1.call-done = f32[256,128,128]{2,1,0:T(8,128)} async-done(((f32[2,128,128]{2,1,0:T(8,128)}), f32[256,128,128]{2,1,0:T(8,128)}) %all-gather.13.cloned.1.call-update) | async-done | bytes 16777232 | tf_op jit(solution)/shard_map/all_gather | solution.py:14
  727.8 11.6 %rev.6 = f32[128,2,128,128]{3,2,1,0:T(8,128)} reverse(f32[128,2,128,128]{3,2,1,0:T(8,128)} %bitcast.334), dimensions={0} | reverse | bytes 33554432 | tf_op jit(solution)/shard_map/rev | solution.py:16
  739.4 175.8 %all-gather.15.cloned.1.call-done = f32[256,128,128]{2,1,0:T(8,128)} async-done(((f32[2,128,128]{2,1,0:T(8,128)}), f32[256,128,128]{2,1,0:T(8,128)}) %all-gather.15.cloned.1.call-update) | async-done | bytes 16777232 | tf_op jit(solution)/shard_map/all_gather | solution.py:14
  915.3 11.8 %rev.7 = f32[128,2,128,128]{3,2,1,0:T(8,128)} reverse(f32[128,2,128,128]{3,2,1,0:T(8,128)} %bitcast.335), dimensions={0} | reverse | bytes 33554432 | tf_op jit(solution)/shard_map/rev | solution.py:16
  927.0 138.1 %while.33 = (s32[]{:T(128)}, f32[2,128,128]{2,1,0:T(8,128)S(1)}, f32[2,128,128]{2,1,0:T(8,128)S(1)}, s32[]{:T(128)}, f32[128,2,128,128]{3,2,1,0:T(8,128)}, /*ind...) while((s32[]{:T(128)}, f32[2,128,128]{2,1,0:T(8,128)S(1)}, f32[2,128,128]{2,1,0:T(8,128)S(1)}, ...), condition=%wide.region_11.12_spmd.clone, body=%wide.region_10.11_spmd.clone.sunk | while | flops 196612 | bytes 786549 | solution.py:26
  (284 shorter events, 253.6 us)
Async XLA Ops:
  7.2 35.3 %copy-start = (bf16[256,2048]{1,0:T(8,128)(2,1)S(1)}, bf16[256,2048]{1,0:T(8,128)(2,1)}, u32[]{:S(2)}) copy-start(bf16[256,2048]{1,0:T(8,128)(2,1)} %param.14) | copy-start | bytes 3145732
  7.2 539.1 %copy-start.2 = (f32[128,256]{1,0:T(8,128)S(1)}, f32[128,256]{1,0:T(8,128)}, u32[]{:S(2)}) copy-start(f32[128,256]{1,0:T(8,128)} %param.11) | copy-start | bytes 393220
  7.2 539.5 %copy-start.4 = (f32[2]{0:T(128)S(1)}, f32[2]{0:T(128)}, u32[]{:S(2)}) copy-start(f32[2]{0:T(128)} %param.15) | copy-start | bytes 28
  7.2 202.3 %all-gather.11.cloned.1.call-start = ((), (), s32[]{:S(2)}) async-start(), calls=%async_computation.1 | async-start | bytes 16908288 | tf_op jit(solution)/shard_map/all_gather | solution.py:14
  9.4 387.7 %all-gather.9.cloned.1.call-start = ((), (), s32[]{:S(2)}) async-start(), calls=%async_computation | async-start | bytes 16908288 | tf_op jit(solution)/shard_map/all_gather | solution.py:14
  11.5 716.3 %all-gather.13.cloned.1.call-start = ((), (), s32[]{:S(2)}) async-start(), calls=%async_computation.2 | async-start | bytes 16908288 | tf_op jit(solution)/shard_map/all_gather | solution.py:14
  544.8 370.5 %all-gather.15.cloned.1.call-start = ((), (), s32[]{:S(2)}) async-start(), calls=%async_computation.3 | async-start | bytes 16908288 | tf_op jit(solution)/shard_map/all_gather | solution.py:14
  915.3 153.3 %copy-start.1 = (bf16[256,2048]{1,0:T(8,128)(2,1)S(1)}, bf16[256,2048]{1,0:T(8,128)(2,1)}, u32[]{:S(2)}) copy-start(bf16[256,2048]{1,0:T(8,128)(2,1)} %param.14) | copy-start | bytes 3145732
  915.3 149.9 %copy-start.3 = (f32[128,256]{1,0:T(8,128)S(1)}, f32[128,256]{1,0:T(8,128)}, u32[]{:S(2)}) copy-start(f32[128,256]{1,0:T(8,128)} %param.12) | copy-start | bytes 393220
Sparse Core Ops, SparseCore 0:
  12.7 196.7 all-gather.10
  214.2 182.8 all-gather.8
  544.9 182.8 all-gather.12
  732.3 182.8 all-gather.14
where the time goes:
time: 1080 us
  waiting for transfers between devices  705 us (65%)
  other arithmetic  271 us (25%)
  blocking collectives  27.3 us (3%)
  local copies, waits for them, and re-layouts  26.7 us (2%)
  matrix products  24.9 us (2%)
  between operations  14.1 us (1%)
    all_gather x4, waiting for transfers between devices, carried_in(): pieces = jax.tree.map(lambda part: lax.all_gather(part, axis), value)  705 us
    select_n x254, other arithmetic, hop(): jnp.where(position < mine, new, old)  270 us
    all_gather x1, blocking collectives, on_device(): lax.all_gather(out_grad, 'head', axis=1, tiled=True)  27.3 us
    rev x2, local copies, waits for them, and re-layouts, carried_in(): pieces = jax.tree.map(lambda part: part[::-1], pieces)  23.4 us
  transfers between devices with their start and end apart: 4, of which 4 were waited for; matrix products, arithmetic and copies ran while one was open for 2% of the time, Pallas kernels for 0%

commit v1 on v0

v1 whole, which is shorter than its diff:
```python
import functools

import jax
import jax.numpy as jnp
from jax import lax
from jax.experimental import pallas as pl
from jax.experimental.pallas import tpu as pltpu
from jax.sharding import PartitionSpec as P

EPS = 1e-06
F32 = jnp.float32
BF16 = jnp.bfloat16


def halves(a):
    high = a.astype(BF16)
    return high, (a - high.astype(F32)).astype(BF16)


def left(a):
    return jnp.concatenate(halves(a), axis=1)


def right(b):
    row = jnp.concatenate(halves(b), axis=1)
    return jnp.concatenate([row, row], axis=0)


def right_t(b):
    column = jnp.concatenate(halves(b), axis=0)
    return jnp.concatenate([column, column], axis=1)


def fold(wide):
    n = wide.shape[1] // 2
    return wide[:, :n] + wide[:, n:]


def mul(a2, b2):
    return fold(lax.dot_general(a2, b2, (((1,), (0,)), ((), ())), preferred_element_type=F32))


def mul_t(a2, b2):
    return fold(lax.dot_general(a2, b2, (((1,), (1,)), ((), ())), preferred_element_type=F32))


def row_dot(a, b):
    return jnp.sum(a * b, axis=-1, keepdims=True)


def column_block(ref, h, size):
    return ref[:, h * size : (h + 1) * size]


def state_kernel(k_ref, v_ref, out_ref, *, heads, size):
    for h in range(heads):
        k = column_block(k_ref, h, size)
        v = column_block(v_ref, h, size)
        key_side = right(k)
        out_ref[:, h * size : (h + 1) * size] = mul(left(k.T), key_side)
        out_ref[:, (heads + h) * size : (heads + h + 1) * size] = mul(left(v.T), key_side)


def scan_kernel(x_ref, out_ref, *, backward):
    x = x_ref[...]
    count = x.shape[0]
    rows = lax.broadcasted_iota(jnp.int32, (count, count), 0)
    cols = lax.broadcasted_iota(jnp.int32, (count, count), 1)
    earlier = ((cols > rows) if backward else (cols < rows)).astype(F32).astype(BF16)
    total = None
    rest = x
    for _ in range(3):
        piece = rest.astype(BF16)
        rest = rest - piece.astype(F32)
        part = lax.dot_general(earlier, piece, (((1,), (0,)), ((), ())), preferred_element_type=F32)
        total = part if total is None else total + part
    out_ref[...] = total


def main_kernel(
    ridge_ref, q_ref, k_ref, v_ref, do_ref, state_ref,
    gq_ref, gk_ref, gv_ref, out_ref, *, heads, size,
):
    tokens = q_ref.shape[0]
    rows = lax.broadcasted_iota(jnp.int32, (tokens, tokens), 0)
    cols = lax.broadcasted_iota(jnp.int32, (tokens, tokens), 1)
    mask = rows >= cols
    each = range(heads)

    def masked(scores):
        return jnp.where(mask, scores, 0.0)

    q = [column_block(q_ref, h, size) for h in each]
    k = [column_block(k_ref, h, size) for h in each]
    v = [column_block(v_ref, h, size) for h in each]
    do = [column_block(do_ref, h, size) for h in each]
    cov = [right(column_block(state_ref, h, size)) for h in each]
    valkey = [right(column_block(state_ref, heads + h, size)) for h in each]
    ridge = [ridge_ref[h] for h in each]
    k_plain = [right(k[h]) for h in each]
    k_turned = [right_t(k[h]) for h in each]

    def apply_matrix(p):
        p2 = [left(p[h]) for h in each]
        scores = [masked(mul_t(p2[h], k_turned[h])) for h in each]
        carried = [mul(p2[h], cov[h]) for h in each]
        image = [mul(left(scores[h]), k_plain[h]) + carried[h] + ridge[h] * p[h] for h in each]
        return scores, image

    s0, a0 = apply_matrix(q)
    do2 = [left(do[h]) for h in each]
    sw = [masked(mul_t(do2[h], right_t(v[h]))) for h in each]
    xb = [mul(left(sw[h]), k_plain[h]) + mul(do2[h], valkey[h]) for h in each]

    n0 = [row_dot(q[h], q[h]) for h in each]
    d0 = [row_dot(q[h], a0[h]) + EPS for h in each]
    al0 = [n0[h] / d0[h] for h in each]
    r1 = [q[h] - al0[h] * a0[h] for h in each]
    n1 = [row_dot(r1[h], r1[h]) for h in each]
    beta = [n1[h] / (n0[h] + EPS) for h in each]
    p1 = [r1[h] + beta[h] * q[h] for h in each]
    s1, a1 = apply_matrix(p1)
    d1 = [row_dot(p1[h], a1[h]) + EPS for h in each]
    al1 = [n1[h] / d1[h] for h in each]

    al1b = [row_dot(xb[h], p1[h]) for h in each]
    n1b = [al1b[h] / d1[h] for h in each]
    d1b = [-n1b[h] * al1[h] for h in each]
    p1b = [al1[h] * xb[h] + (2.0 * d1b[h]) * a1[h] for h in each]
    betab = [row_dot(p1b[h], q[h]) for h in each]
    n1b = [n1b[h] + betab[h] / (n0[h] + EPS) for h in each]
    n0b = [-betab[h] * beta[h] / (n0[h] + EPS) for h in each]
    r1b = [p1b[h] + (2.0 * n1b[h]) * r1[h] for h in each]
    al0b = [row_dot(xb[h], q[h]) - row_dot(r1b[h], a0[h]) for h in each]
    d0b = [-al0b[h] * al0[h] / d0[h] for h in each]
    n0b = [n0b[h] + al0b[h] / d0[h] for h in each]
    a0b = [d0b[h] * q[h] - al0[h] * r1b[h] for h in each]
    s2, back = apply_matrix(a0b)

    for h in each:
        here = slice(h * size, (h + 1) * size)
        x = al0[h] * q[h] + al1[h] * p1[h]
        sx = al0[h] * s0[h] + al1[h] * s1[h]
        c1 = (2.0 * d1b[h]) * p1[h]
        gq_ref[:, here] = (
            beta[h] * p1b[h] + al0[h] * xb[h] + d0b[h] * a0[h] + back[h] + r1b[h]
            + (2.0 * n0b[h]) * q[h]
        )
        x2, q2, p2, a2, do2_right = right(x), right(q[h]), right(p1[h]), right(a0b[h]), right(do[h])
        c2 = right(c1)
        gk_ref[:, here] = (
            mul(left(sw[h].T), x2) + mul(left(s1[h].T), c2)
            + mul(left(s0[h].T), a2) + mul(left(s2[h].T), q2)
        )
        gv_ref[:, here] = mul(left(sx.T), do2_right)
        out_ref[:, here] = (
            mul(left(c1.T), p2) + mul(left(a0b[h].T), q2) + mul(left(q[h].T), a2)
        )
        out_ref[:, (heads + h) * size : (heads + h + 1) * size] = mul(left(do[h].T), x2)


def final_kernel(k_ref, v_ref, gk_ref, gv_ref, state_ref, gk_out, gv_out, *, heads, size):
    for h in range(heads):
        here = slice(h * size, (h + 1) * size)
        cov = column_block(state_ref, h, size)
        valkey = column_block(state_ref, heads + h, size)
        k2 = left(k_ref[:, here])
        v2 = left(v_ref[:, here])
        gk_out[:, here] = gk_ref[:, here] + mul(k2, right(cov)) + mul(v2, right(valkey))
        gv_out[:, here] = gv_ref[:, here] + mul_t(k2, right_t(valkey))


VMEM = pl.BlockSpec(memory_space=pltpu.VMEM)
SMEM = pl.BlockSpec(memory_space=pltpu.SMEM)
PARAMS = pltpu.CompilerParams(vmem_limit_bytes=32 * 1024 * 1024)


def call(kernel, in_specs, out_shape):
    out_specs = VMEM if not isinstance(out_shape, tuple) else (VMEM,) * len(out_shape)
    return pl.pallas_call(
        kernel, in_specs=in_specs, out_specs=out_specs, out_shape=out_shape, compiler_params=PARAMS
    )


def scan_over(state, backward):
    count = lax.axis_size("seq")
    width = state.shape[0] * state.shape[1] // count
    parts = lax.all_to_all(state.reshape(count, width), "seq", 0, 0, tiled=True)
    sums = call(
        functools.partial(scan_kernel, backward=backward),
        [VMEM],
        jax.ShapeDtypeStruct(parts.shape, F32),
    )(parts)
    return lax.all_to_all(sums, "seq", 0, 0, tiled=True).reshape(state.shape)


def on_device(queries, keys, values, out_grad, w_out, ridge):
    tokens, columns = queries.shape
    heads = ridge.shape[0]
    size = columns // heads
    sizes = dict(heads=heads, size=size)
    local = jax.ShapeDtypeStruct((tokens, columns), F32)
    state_shape = jax.ShapeDtypeStruct((size, 2 * columns), F32)

    states = call(functools.partial(state_kernel, **sizes), [VMEM] * 2, state_shape)(keys, values)
    before = scan_over(states, False)
    d_out = lax.dot_general(
        lax.all_gather(out_grad, "head", axis=1, tiled=True),
        w_out,
        (((1,), (1,)), ((), ())),
        preferred_element_type=F32,
    )
    grad_q, grad_k, grad_v, adjoints = call(
        functools.partial(main_kernel, **sizes),
        [SMEM] + [VMEM] * 5,
        (local, local, local, state_shape),
    )(ridge, queries, keys, values, d_out, before)
    later = scan_over(adjoints, True)
    grad_k, grad_v = call(
        functools.partial(final_kernel, **sizes), [VMEM] * 5, (local, local)
    )(keys, values, grad_k, grad_v, later)
    return grad_q, grad_k, grad_v


def solution(mesh):
    rows = P("seq", "head")
    return jax.shard_map(
        on_device,
        mesh=mesh,
        in_specs=(rows, rows, rows, rows, P("head", None), P("head")),
        out_specs=(rows, rows, rows),
        check_vma=False,
    )
```

time: 1080 us -> 153 us (0.14)
  the two profiles are of different devices: /device:TPU:1 before, /device:TPU:2 now
where the time goes in v1:
time: 153 us
  blocking collectives  126 us (82%)
  waiting for transfers between devices  9.75 us (6%)
  starting transfers between devices  6.29 us (4%)
  Pallas kernels  4.64 us (3%)
  local copies, waits for them, and re-layouts  4.4 us (3%)
    all_to_all x2, blocking collectives, scan_over(): parts = lax.all_to_all(state.reshape(count, width), 'seq', 0, 0, tiled=True)  83.5 us
    all_to_all x1, blocking collectives, scan_over(): return lax.all_to_all(sums, 'seq', 0, 0, tiled=True).reshape(state.shape)  29.6 us
    all_gather x1, blocking collectives, on_device(): lax.all_gather(out_grad, 'head', axis=1, tiled=True)  13.2 us
    all_to_all x1, waiting for transfers between devices, scan_over(): return lax.all_to_all(sums, 'seq', 0, 0, tiled=True).reshape(state.shape)  9.75 us
    all_to_all x1, starting transfers between devices, scan_over(): return lax.all_to_all(sums, 'seq', 0, 0, tiled=True).reshape(state.shape)  6.29 us
  transfers between devices with their start and end apart: 1, of which 1 were waited for; matrix products, arithmetic and copies ran while one was open for 0% of the time, Pallas kernels for 0%

profile of v1, /device:TPU:2, one launch (start us, length us, event | category | flops | bytes accessed | tf_op | source)
XLA Modules:
  0.0 152.6 jit_solution(12821683806474764440)
XLA Ops:
  0.6 0.0 copy-start
  0.6 0.0 copy-start.1
  0.7 1.0 copy-done.1
  1.6 0.0 copy-start.3
  1.6 0.9 copy-done.3
  2.5 0.3 shard_map.85
  2.8 0.3 copy.9
  3.1 50.1 %all_to_all.44 = f32[128,1,512]{2,1,0:T(1,128)S(1)} all-to-all(f32[128,1,512]{2,1,0:T(1,128)S(1)} %copy.9), channel_id=1, replica_groups=mesh['seq'=128,'head'=8] {'seq'}, dimensions={0} | all-to-all | bytes 524288 | tf_op jit(solution)/shard_map/all_to_all | solution.py:188
  53.2 0.3 shard_map.86
  53.5 1.0 copy.10
  54.5 0.0 copy-start.7
  54.5 6.3 %all-to-all-start.1 = ((f32[128,1,512]{2,1,0:T(1,128)}), f32[128,1,512]{2,1,0:T(1,128)S(1)}, u32[]{:S(2)}, u32[]{:S(2)}) async-start(f32[128,1,512]{2,1,0:T(1,128)} %copy.10), calls=%async_computation.1 | async-start | bytes 524288 | tf_op jit(solution)/shard_map/all_to_all | solution.py:194
  60.8 0.0 copy-done.7
  60.8 13.2 %all_gather.3 = bf16[128,2048]{1,0:T(8,128)(2,1)S(1)} all-gather(bf16[128,256]{1,0:T(8,128)(2,1)S(1)} %copy-done.7), channel_id=1, replica_groups=mesh['seq'=128,'head'=8] {'head'}, dimensions={1}, use_global_device_ids=true | all-gather | bytes 589824 | tf_op jit(solution)/shard_map/all_gather | solution.py:208
  74.0 0.0 copy-done
  74.0 0.5 fusion.do_ref
  74.4 0.0 copy-start.2
  74.5 0.0 copy-start.4
  74.5 0.0 copy-start.5
  74.5 9.8 %all-to-all-done.1 = f32[128,1,512]{2,1,0:T(1,128)S(1)} async-done(((f32[128,1,512]{2,1,0:T(1,128)}), f32[128,1,512]{2,1,0:T(1,128)S(1)}, u32[]{:S(2)}, u32[]{:S(2)}) %all-to-all-start.1) | async-done | bytes 262176 | tf_op jit(solution)/shard_map/all_to_all | solution.py:194
  84.3 0.0 copy-start.6
  84.3 0.0 copy-done.2
  84.3 0.0 copy-done.4
  84.3 0.0 copy-done.5
  84.3 0.6 copy-done.6
  84.9 2.8 %shard_map.87 = (f32[128,256]{1,0:T(8,128)}, f32[128,256]{1,0:T(8,128)S(1)}, f32[128,256]{1,0:T(8,128)S(1)}, f32[128,512]{1,0:T(8,128)S(1)}) custom-call(f32[2]{0:T(128)S(1)} %copy-done.6, f32[128,256]{1,0:T(8,128)S(1)} %copy-done.5, f32[128,256]{1,0:T(8,128)S(1)} %copy-done.2, f32[128,256]{1,0:T(8,128)S(1)} %copy-done.4, f32[128,256]{1,0:T(8,128)S(1)} %fusion.do_ref, ...), custom_call_target="tpu_custom_call" | custom-call | tf_op jit(solution)/shard_map/pallas_call | solution.py:213
  87.7 0.3 copy.11
  88.0 33.4 %all_to_all.45 = f32[128,1,512]{2,1,0:T(1,128)S(1)} all-to-all(f32[128,1,512]{2,1,0:T(1,128)S(1)} %copy.11), channel_id=1, replica_groups=mesh['seq'=128,'head'=8] {'seq'}, dimensions={0} | all-to-all | bytes 524288 | tf_op jit(solution)/shard_map/all_to_all | solution.py:188
  121.4 0.3 shard_map.88
  121.7 0.3 copy.12
  122.0 29.6 %all_to_all.46 = f32[128,1,512]{2,1,0:T(1,128)S(1)} all-to-all(f32[128,1,512]{2,1,0:T(1,128)S(1)} %copy.12), channel_id=1, replica_groups=mesh['seq'=128,'head'=8] {'seq'}, dimensions={0} | all-to-all | bytes 524288 | tf_op jit(solution)/shard_map/all_to_all | solution.py:194
  151.6 1.0 shard_map.89
  (4 shorter events, 0.1 us)
Async XLA Ops:
  0.6 73.3 %copy-start = (bf16[256,2048]{1,0:T(8,128)(2,1)S(1)}, bf16[256,2048]{1,0:T(8,128)(2,1)}, u32[]{:S(2)}) copy-start(bf16[256,2048]{1,0:T(8,128)(2,1)} %param.10) | copy-start | bytes 3145732
  0.6 1.0 copy-start.1
  1.6 0.9 copy-start.3
  54.5 6.3 %copy-start.7 = (bf16[128,256]{1,0:T(8,128)(2,1)S(1)}, bf16[128,256]{1,0:T(8,128)(2,1)}, u32[]{:S(2)}) copy-start(bf16[128,256]{1,0:T(8,128)(2,1)} %param.9) | copy-start | bytes 196612
  54.5 29.8 %all-to-all-start.1 = ((f32[128,1,512]{2,1,0:T(1,128)}), f32[128,1,512]{2,1,0:T(1,128)S(1)}, u32[]{:S(2)}, u32[]{:S(2)}) async-start(f32[128,1,512]{2,1,0:T(1,128)} %copy.10), calls=%async_computation.1 | async-start | bytes 524288 | tf_op jit(solution)/shard_map/all_to_all | solution.py:194
  74.4 9.8 %copy-start.2 = (f32[128,256]{1,0:T(8,128)S(1)}, f32[128,256]{1,0:T(8,128)}, u32[]{:S(2)}) copy-start(f32[128,256]{1,0:T(8,128)} %k_ref.5) | copy-start | bytes 393220
  74.5 9.8 %copy-start.4 = (f32[128,256]{1,0:T(8,128)S(1)}, f32[128,256]{1,0:T(8,128)}, u32[]{:S(2)}) copy-start(f32[128,256]{1,0:T(8,128)} %v_ref.5) | copy-start | bytes 393220
  74.5 9.8 %copy-start.5 = (f32[128,256]{1,0:T(8,128)S(1)}, f32[128,256]{1,0:T(8,128)}, u32[]{:S(2)}) copy-start(f32[128,256]{1,0:T(8,128)} %q_ref.1) | copy-start | bytes 393220
  84.3 0.7 copy-start.6

commit v2 on v1

--- a/solution.py
+++ b/solution.py
@@ -52,20 +52,58 @@
     return ref[:, h * size : (h + 1) * size]
 
 
+def square_iota(size):
+    rows = lax.broadcasted_iota(jnp.int32, (size, size), 0)
+    return rows, lax.broadcasted_iota(jnp.int32, (size, size), 1)
+
+
+def pack(cov, valkey, out_ref):
+    parts, size = out_ref.shape[0], cov[0].shape[0]
+    each = size // parts
+    rows, cols = square_iota(size)
+    both = jnp.where(rows <= cols, cov[0], cov[1])
+    for i, matrix in enumerate((both, *valkey)):
+        for r in range(each):
+            at = (i * each + r) * size
+            out_ref[:, at : at + size] = matrix[r * parts : (r + 1) * parts]
+    diagonal = jnp.sum(jnp.where(rows == cols, cov[1], 0.0), axis=0, keepdims=True)
+    owner = lax.broadcasted_iota(jnp.int32, (parts, size), 0)
+    lane = lax.broadcasted_iota(jnp.int32, (parts, size), 1)
+    mine = (lane >= owner * each) & (lane < (owner + 1) * each)
+    out_ref[:, 3 * each * size :] = jnp.where(mine, diagonal, 0.0)
+
+
+def unpack(ref, size):
+    parts = ref.shape[0]
+    each = size // parts
+
+    def matrix(i):
+        pieces = [ref[:, at * size : (at + 1) * size] for at in range(i * each, (i + 1) * each)]
+        return jnp.concatenate(pieces, axis=0)
+
+    both = matrix(0)
+    turned = both.T
+    rows, cols = square_iota(size)
+    diagonal = jnp.sum(ref[:, 3 * each * size :], axis=0, keepdims=True)
+    first = jnp.where(rows <= cols, both, turned)
+    second = jnp.where(rows > cols, both, jnp.where(rows == cols, diagonal, turned))
+    return (first, second), (matrix(1), matrix(2))
+
+
 def state_kernel(k_ref, v_ref, out_ref, *, heads, size):
+    cov, valkey = [], []
     for h in range(heads):
         k = column_block(k_ref, h, size)
         v = column_block(v_ref, h, size)
         key_side = right(k)
-        out_ref[:, h * size : (h + 1) * size] = mul(left(k.T), key_side)
-        out_ref[:, (heads + h) * size : (heads + h + 1) * size] = mul(left(v.T), key_side)
-
-
-def scan_kernel(x_ref, out_ref, *, backward):
+        cov.append(mul(left(k.T), key_side))
+        valkey.append(mul(left(v.T), key_side))
+    pack(cov, valkey, out_ref)
+
+
+def inner_kernel(group_ref, x_ref, sums_ref, total_ref, *, backward):
     x = x_ref[...]
-    count = x.shape[0]
-    rows = lax.broadcasted_iota(jnp.int32, (count, count), 0)
-    cols = lax.broadcasted_iota(jnp.int32, (count, count), 1)
+    rows, cols = square_iota(x.shape[0])
     earlier = ((cols > rows) if backward else (cols < rows)).astype(F32).astype(BF16)
     total = None
     rest = x
@@ -74,7 +112,15 @@
         rest = rest - piece.astype(F32)
         part = lax.dot_general(earlier, piece, (((1,), (0,)), ((), ())), preferred_element_type=F32)
         total = part if total is None else total + part
-    out_ref[...] = total
+    sums_ref[...] = total
+    group = group_ref[0]
+    reader = lax.broadcasted_iota(jnp.int32, total_ref.shape, 0)
+    reads = (reader < group) if backward else (reader > group)
+    total_ref[...] = jnp.where(reads, jnp.sum(x, axis=0, keepdims=True), 0.0)
+
+
+def outer_kernel(sums_ref, totals_ref, out_ref):
+    out_ref[...] = sums_ref[...] + jnp.sum(totals_ref[...], axis=0, keepdims=True)
 
 
 def main_kernel(
@@ -94,9 +140,8 @@
     k = [column_block(k_ref, h, size) for h in each]
     v = [column_block(v_ref, h, size) for h in each]
     do = [column_block(do_ref, h, size) for h in each]
-    cov = [right(column_block(state_ref, h, size)) for h in each]
-    valkey = [right(column_block(state_ref, heads + h, size)) for h in each]
-    ridge = [ridge_ref[h] for h in each]
+    cov, valkey = [[right(m) for m in pair] for pair in unpack(state_ref, size)]
+    ridge = [column_block(ridge_ref, h, size) for h in each]
     k_plain = [right(k[h]) for h in each]
     k_turned = [right_t(k[h]) for h in each]
 
@@ -137,6 +182,7 @@
     a0b = [d0b[h] * q[h] - al0[h] * r1b[h] for h in each]
     s2, back = apply_matrix(a0b)
 
+    cov_out, valkey_out = [], []
     for h in each:
         here = slice(h * size, (h + 1) * size)
         x = al0[h] * q[h] + al1[h] * p1[h]
@@ -153,21 +199,20 @@
             + mul(left(s0[h].T), a2) + mul(left(s2[h].T), q2)
         )
         gv_ref[:, here] = mul(left(sx.T), do2_right)
-        out_ref[:, here] = (
-            mul(left(c1.T), p2) + mul(left(a0b[h].T), q2) + mul(left(q[h].T), a2)
-        )
-        out_ref[:, (heads + h) * size : (heads + h + 1) * size] = mul(left(do[h].T), x2)
+        turned = mul(left(a0b[h].T), q2)
+        cov_out.append(mul(left(c1.T), p2) + turned + turned.T)
+        valkey_out.append(mul(left(do[h].T), x2))
+    pack(cov_out, valkey_out, out_ref)
 
 
 def final_kernel(k_ref, v_ref, gk_ref, gv_ref, state_ref, gk_out, gv_out, *, heads, size):
+    cov, valkey = unpack(state_ref, size)
     for h in range(heads):
         here = slice(h * size, (h + 1) * size)
-        cov = column_block(state_ref, h, size)
-        valkey = column_block(state_ref, heads + h, size)
         k2 = left(k_ref[:, here])
         v2 = left(v_ref[:, here])
-        gk_out[:, here] = gk_ref[:, here] + mul(k2, right(cov)) + mul(v2, right(valkey))
-        gv_out[:, here] = gv_ref[:, here] + mul_t(k2, right_t(valkey))
+        gk_out[:, here] = gk_ref[:, here] + mul(k2, right(cov[h])) + mul(v2, right(valkey[h]))
+        gv_out[:, here] = gv_ref[:, here] + mul_t(k2, right_t(valkey[h]))
 
 
 VMEM = pl.BlockSpec(memory_space=pltpu.VMEM)
@@ -182,16 +227,28 @@
     )
 
 
-def scan_over(state, backward):
-    count = lax.axis_size("seq")
-    width = state.shape[0] * state.shape[1] // count
-    parts = lax.all_to_all(state.reshape(count, width), "seq", 0, 0, tiled=True)
-    sums = call(
-        functools.partial(scan_kernel, backward=backward),
-        [VMEM],
-        jax.ShapeDtypeStruct(parts.shape, F32),
-    )(parts)
-    return lax.all_to_all(sums, "seq", 0, 0, tiled=True).reshape(state.shape)
+def split_blocks(count):
+    inner = 16 if count % 16 == 0 and count > 16 else max(1, count // 4)
+    return inner, count // inner
+
+
+def scan_over(state, backward, beside):
+    inner, groups = split_blocks(lax.axis_size("seq"))
+    within = [[g * inner + i for i in range(inner)] for g in range(groups)]
+    across = [[g * inner + i for g in range(groups)] for i in range(inner)]
+
+    def exchange(array, members):
+        return lax.all_to_all(array, "seq", 0, 0, axis_index_groups=members, tiled=True)
+
+    received, beside = lax.optimization_barrier((exchange(state, within), beside))
+    same = jax.ShapeDtypeStruct(state.shape, F32)
+    sums, totals = call(
+        functools.partial(inner_kernel, backward=backward),
+        [SMEM, VMEM],
+        (same, jax.ShapeDtypeStruct((groups, state.shape[1]), F32)),
+    )(beside[0], received)
+    result = call(outer_kernel, [VMEM, VMEM], same)(sums, exchange(totals, across))
+    return exchange(result, within), beside
 
 
 def on_device(queries, keys, values, out_grad, w_out, ridge):
@@ -200,22 +257,27 @@
     size = columns // heads
     sizes = dict(heads=heads, size=size)
     local = jax.ShapeDtypeStruct((tokens, columns), F32)
-    state_shape = jax.ShapeDtypeStruct((size, 2 * columns), F32)
+    parts = split_blocks(lax.axis_size("seq"))[0]
+    state_shape = jax.ShapeDtypeStruct((parts, (3 * size // parts + 1) * size), F32)
 
     states = call(functools.partial(state_kernel, **sizes), [VMEM] * 2, state_shape)(keys, values)
-    before = scan_over(states, False)
     d_out = lax.dot_general(
         lax.all_gather(out_grad, "head", axis=1, tiled=True),
         w_out,
         (((1,), (1,)), ((), ())),
         preferred_element_type=F32,
     )
+    group = (lax.axis_index("seq") // split_blocks(lax.axis_size("seq"))[0]).astype(jnp.int32)
+    ridge_row = jnp.repeat(ridge, size)[None]
+    before, (group, d_out, ridge_row) = scan_over(
+        states, False, (group.reshape(1), d_out, ridge_row)
+    )
     grad_q, grad_k, grad_v, adjoints = call(
         functools.partial(main_kernel, **sizes),
-        [SMEM] + [VMEM] * 5,
+        [VMEM] * 6,
         (local, local, local, state_shape),
-    )(ridge, queries, keys, values, d_out, before)
-    later = scan_over(adjoints, True)
+    )(ridge_row, queries, keys, values, d_out, before)
+    later, _ = scan_over(adjoints, True, (group,))
     grad_k, grad_v = call(
         functools.partial(final_kernel, **sizes), [VMEM] * 5, (local, local)
     )(keys, values, grad_k, grad_v, later)

time: 153 us -> 140 us (0.915)
  blocking collectives: 126 us -> 107 us
  starting transfers between devices: 6.29 us -> 19 us
  waiting for transfers between devices: 9.75 us -> 2.98 us
    all_to_all x3 -> x5, blocking collectives: 113 us -> 93.6 us  [exchange(): lax.all_to_all(array, 'seq', 0, 0, axis_index_groups=members, tiled=True)]
    all_to_all x1, starting transfers between devices: 6.29 us -> 19 us  [exchange(): lax.all_to_all(array, 'seq', 0, 0, axis_index_groups=members, tiled=True)]
    all_to_all x1, waiting for transfers between devices: 9.75 us -> 2.98 us  [exchange(): lax.all_to_all(array, 'seq', 0, 0, axis_index_groups=members, tiled=True)]
    unnamed x20 -> x22, local copies, waits for them, and re-layouts: 2.61 us -> 3.64 us
    pallas_call x3 -> x5, Pallas kernels: 3.37 us -> 2.58 us  [the longest x1 2.07 us: on_device(): call(functools.partial(main_kernel, **sizes), [VMEM] * 6, (local, local,...]
where the time goes in v2:
time: 140 us; the launch traced here: 139 us
  blocking collectives  107 us (76%)
  starting transfers between devices  19 us (14%)
  local copies, waits for them, and re-layouts  5.46 us (4%)
  Pallas kernels  3.91 us (3%)
  waiting for transfers between devices  2.98 us (2%)
    all_to_all x5, blocking collectives, exchange(): lax.all_to_all(array, 'seq', 0, 0, axis_index_groups=members, tiled=True)  93.6 us
    all_to_all x1, starting transfers between devices, exchange(): lax.all_to_all(array, 'seq', 0, 0, axis_index_groups=members, tiled=True)  19 us
    all_gather x1, blocking collectives, on_device(): lax.all_gather(out_grad, 'head', axis=1, tiled=True)  13.2 us
    unnamed x22, local copies, waits for them, and re-layouts  3.64 us
    all_to_all x1, waiting for transfers between devices, exchange(): lax.all_to_all(array, 'seq', 0, 0, axis_index_groups=members, tiled=True)  2.98 us
  transfers between devices with their start and end apart: 1, of which 1 were waited for; matrix products, arithmetic and copies ran while one was open for 0% of the time, Pallas kernels for 0%

profile of v2, /device:TPU:2, one launch (start us, length us, event | category | flops | bytes accessed | tf_op | source)
XLA Modules:
  0.0 139.3 jit_solution(14828774387614690822)
XLA Ops:
  0.6 0.0 copy-start
  0.6 0.0 copy-start.1
  0.7 1.0 copy-done.1
  1.6 0.0 copy-start.3
  1.6 0.9 copy-done.3
  2.5 0.3 shard_map.85
  2.8 0.9 copy.9
  3.7 0.0 copy-start.6
  3.7 19.0 %all-to-all-start = ((f32[16,1,3200]{2,1,0:T(1,128)}), f32[16,1,3200]{2,1,0:T(1,128)S(1)}, u32[]{:S(2)}, u32[]{:S(2)}) async-start(f32[16,1,3200]{2,1,0:T(1,128)} %copy.9), calls=%async_computation | async-start | bytes 409600 | tf_op jit(solution)/shard_map/all_to_all | solution.py:241
  22.8 0.0 copy-done.6
  22.8 13.2 %all_gather.3 = bf16[128,2048]{1,0:T(8,128)(2,1)S(1)} all-gather(bf16[128,256]{1,0:T(8,128)(2,1)S(1)} %copy-done.6), channel_id=1, replica_groups=mesh['seq'=128,'head'=8] {'head'}, dimensions={1}, use_global_device_ids=true | all-gather | bytes 589824 | tf_op jit(solution)/shard_map/all_gather | solution.py:265
  35.9 0.0 copy-done
  35.9 0.5 fusion.do_ref
  36.4 3.0 %all-to-all-done = f32[16,1,3200]{2,1,0:T(1,128)S(1)} async-done(((f32[16,1,3200]{2,1,0:T(1,128)}), f32[16,1,3200]{2,1,0:T(1,128)S(1)}, u32[]{:S(2)}, u32[]{:S(2)}) %all-to-all-start) | async-done | bytes 204832 | tf_op jit(solution)/shard_map/all_to_all | solution.py:241
  39.4 0.0 copy-start.7
  39.4 0.6 copy-done.7
  40.1 0.1 broadcast_in_dim.3
  40.2 0.2 shard_map.86
  40.4 0.1 copy.10
  40.5 15.7 %all_to_all.68 = f32[8,1,3200]{2,1,0:T(1,128)S(1)} all-to-all(f32[8,1,3200]{2,1,0:T(1,128)S(1)} %copy.10), channel_id=1, replica_groups={{0,128,256,384,512,640,768,896},{8,136,264,392,520,648,776,904},{16,144..., dimensions={0} | all-to-all | bytes 204800 | tf_op jit(solution)/shard_map/all_to_all | solution.py:241
  56.2 0.2 copy.11
  56.4 25.0 %all_to_all.69 = f32[16,1,3200]{2,1,0:T(1,128)S(1)} all-to-all(f32[16,1,3200]{2,1,0:T(1,128)S(1)} %copy.11), channel_id=1, replica_groups={{0,8,16,24,32,40,48,56,64,72,80,88,96,104,112,120},{128,136,144,152,160..., dimensions={0} | all-to-all | bytes 409600 | tf_op jit(solution)/shard_map/all_to_all | solution.py:241
  81.5 0.0 copy-start.2
  81.5 0.0 copy-start.4
  81.5 0.0 copy-start.5
  81.5 0.9 copy-done.2
  82.4 0.1 copy-done.4
  82.4 0.1 copy-done.5
  82.5 2.1 %shard_map.88 = (f32[128,256]{1,0:T(8,128)}, f32[128,256]{1,0:T(8,128)S(1)}, f32[128,256]{1,0:T(8,128)S(1)}, f32[16,3200]{1,0:T(8,128)S(1)}) custom-call(f32[1,256]{1,0:T(1,128)S(1)} %bitcast.40, f32[128,256]{1,0:T(8,128)S(1)} %copy-done.5, f32[128,256]{1,0:T(8,128)S(1)} %copy-done.2, f32[128,256]{1,0:T(8,128)S(1)} %copy-done.4, f32[128,256]{1,0:T(8,128)S(1)} %fusion.do_ref, ...), custom_call_target="tpu_custom_call" | custom-call | tf_op jit(solution)/shard_map/pallas_call | solution.py:275
  84.6 0.2 copy.12
  84.8 20.4 %all_to_all.70 = f32[16,1,3200]{2,1,0:T(1,128)S(1)} all-to-all(f32[16,1,3200]{2,1,0:T(1,128)S(1)} %copy.12), channel_id=1, replica_groups={{0,8,16,24,32,40,48,56,64,72,80,88,96,104,112,120},{128,136,144,152,160..., dimensions={0} | all-to-all | bytes 409600 | tf_op jit(solution)/shard_map/all_to_all | solution.py:241
  105.2 0.2 shard_map.89
  105.4 0.1 copy.13
  105.5 11.8 %all_to_all.71 = f32[8,1,3200]{2,1,0:T(1,128)S(1)} all-to-all(f32[8,1,3200]{2,1,0:T(1,128)S(1)} %copy.13), channel_id=1, replica_groups={{0,128,256,384,512,640,768,896},{8,136,264,392,520,648,776,904},{16,144..., dimensions={0} | all-to-all | bytes 204800 | tf_op jit(solution)/shard_map/all_to_all | solution.py:241
  117.4 0.2 copy.14
  117.6 20.7 %all_to_all.72 = f32[16,1,3200]{2,1,0:T(1,128)S(1)} all-to-all(f32[16,1,3200]{2,1,0:T(1,128)S(1)} %copy.14), channel_id=1, replica_groups={{0,8,16,24,32,40,48,56,64,72,80,88,96,104,112,120},{128,136,144,152,160..., dimensions={0} | all-to-all | bytes 409600 | tf_op jit(solution)/shard_map/all_to_all | solution.py:241
  138.3 1.0 shard_map.91
  (8 shorter events, 0.1 us)
Async XLA Ops:
  0.6 35.3 %copy-start = (bf16[256,2048]{1,0:T(8,128)(2,1)S(1)}, bf16[256,2048]{1,0:T(8,128)(2,1)}, u32[]{:S(2)}) copy-start(bf16[256,2048]{1,0:T(8,128)(2,1)} %param.10) | copy-start | bytes 3145732
  0.6 1.0 copy-start.1
  1.6 0.9 copy-start.3
  3.7 19.0 %copy-start.6 = (bf16[128,256]{1,0:T(8,128)(2,1)S(1)}, bf16[128,256]{1,0:T(8,128)(2,1)}, u32[]{:S(2)}) copy-start(bf16[128,256]{1,0:T(8,128)(2,1)} %param.9) | copy-start | bytes 196612
  3.7 35.7 %all-to-all-start = ((f32[16,1,3200]{2,1,0:T(1,128)}), f32[16,1,3200]{2,1,0:T(1,128)S(1)}, u32[]{:S(2)}, u32[]{:S(2)}) async-start(f32[16,1,3200]{2,1,0:T(1,128)} %copy.9), calls=%async_computation | async-start | bytes 409600 | tf_op jit(solution)/shard_map/all_to_all | solution.py:241
  39.4 0.7 copy-start.7
  81.5 0.9 copy-start.2
  81.5 1.0 copy-start.4
  81.5 1.0 copy-start.5

commit v3 on v2

--- a/solution.py
+++ b/solution.py
@@ -55,6 +55,14 @@
 def square_iota(size):
     rows = lax.broadcasted_iota(jnp.int32, (size, size), 0)
     return rows, lax.broadcasted_iota(jnp.int32, (size, size), 1)
+
+
+def put(ref, at, block):
+    columns = slice(at, at + block.shape[1])
+    if len(ref.shape) == 3:
+        ref[:, 0, columns] = block
+    else:
+        ref[:, columns] = block
 
 
 def pack(cov, valkey, out_ref):
@@ -64,13 +72,12 @@
     both = jnp.where(rows <= cols, cov[0], cov[1])
     for i, matrix in enumerate((both, *valkey)):
         for r in range(each):
-            at = (i * each + r) * size
-            out_ref[:, at : at + size] = matrix[r * parts : (r + 1) * parts]
+            put(out_ref, (i * each + r) * size, matrix[r * parts : (r + 1) * parts])
     diagonal = jnp.sum(jnp.where(rows == cols, cov[1], 0.0), axis=0, keepdims=True)
     owner = lax.broadcasted_iota(jnp.int32, (parts, size), 0)
     lane = lax.broadcasted_iota(jnp.int32, (parts, size), 1)
     mine = (lane >= owner * each) & (lane < (owner + 1) * each)
-    out_ref[:, 3 * each * size :] = jnp.where(mine, diagonal, 0.0)
+    put(out_ref, 3 * each * size, jnp.where(mine, diagonal, 0.0))
 
 
 def unpack(ref, size):
@@ -123,39 +130,48 @@
     out_ref[...] = sums_ref[...] + jnp.sum(totals_ref[...], axis=0, keepdims=True)
 
 
+def causal(scores):
+    rows, cols = square_iota(scores.shape[0])
+    return jnp.where(rows >= cols, scores, 0.0)
+
+
+def local_kernel(
+    ridge_ref, q_ref, k_ref, v_ref, do_ref,
+    q_out, s0_ref, a0_ref, sw_ref, xb_ref, plain_ref, turned_ref, *, heads, size,
+):
+    q_out[...] = q_ref[...]
+    for h in range(heads):
+        here = slice(h * size, (h + 1) * size)
+        q, k = q_ref[:, here], k_ref[:, here]
+        plain, turned = right(k), right_t(k)
+        plain_ref[h], turned_ref[h] = plain, turned
+        s0 = causal(mul_t(left(q), turned))
+        sw = causal(mul_t(left(do_ref[:, here]), right_t(v_ref[:, here])))
+        s0_ref[:, here], sw_ref[:, here] = s0, sw
+        a0_ref[:, here] = mul(left(s0), plain) + ridge_ref[:, here] * q
+        xb_ref[:, here] = mul(left(sw), plain)
+
+
 def main_kernel(
-    ridge_ref, q_ref, k_ref, v_ref, do_ref, state_ref,
+    ridge_ref, do_ref, q_ref, s0_ref, a0_ref, sw_ref, xb_ref, plain_ref, turned_ref, state_ref,
     gq_ref, gk_ref, gv_ref, out_ref, *, heads, size,
 ):
-    tokens = q_ref.shape[0]
-    rows = lax.broadcasted_iota(jnp.int32, (tokens, tokens), 0)
-    cols = lax.broadcasted_iota(jnp.int32, (tokens, tokens), 1)
-    mask = rows >= cols
     each = range(heads)
-
-    def masked(scores):
-        return jnp.where(mask, scores, 0.0)
-
-    q = [column_block(q_ref, h, size) for h in each]
-    k = [column_block(k_ref, h, size) for h in each]
-    v = [column_block(v_ref, h, size) for h in each]
-    do = [column_block(do_ref, h, size) for h in each]
+    ridge, do, q, s0, sw = (
+        [column_block(ref, h, size) for h in each]
+        for ref in (ridge_ref, do_ref, q_ref, s0_ref, sw_ref)
+    )
     cov, valkey = [[right(m) for m in pair] for pair in unpack(state_ref, size)]
-    ridge = [column_block(ridge_ref, h, size) for h in each]
-    k_plain = [right(k[h]) for h in each]
-    k_turned = [right_t(k[h]) for h in each]
 
     def apply_matrix(p):
         p2 = [left(p[h]) for h in each]
-        scores = [masked(mul_t(p2[h], k_turned[h])) for h in each]
+        scores = [causal(mul_t(p2[h], turned_ref[h])) for h in each]
         carried = [mul(p2[h], cov[h]) for h in each]
-        image = [mul(left(scores[h]), k_plain[h]) + carried[h] + ridge[h] * p[h] for h in each]
+        image = [mul(left(scores[h]), plain_ref[h]) + carried[h] + ridge[h] * p[h] for h in each]
         return scores, image
 
-    s0, a0 = apply_matrix(q)
-    do2 = [left(do[h]) for h in each]
-    sw = [masked(mul_t(do2[h], right_t(v[h]))) for h in each]
-    xb = [mul(left(sw[h]), k_plain[h]) + mul(do2[h], valkey[h]) for h in each]
+    a0 = [column_block(a0_ref, h, size) + mul(left(q[h]), cov[h]) for h in each]
+    xb = [column_block(xb_ref, h, size) + mul(left(do[h]), valkey[h]) for h in each]
 
     n0 = [row_dot(q[h], q[h]) for h in each]
     d0 = [row_dot(q[h], a0[h]) + EPS for h in each]
@@ -217,13 +233,14 @@
 
 VMEM = pl.BlockSpec(memory_space=pltpu.VMEM)
 SMEM = pl.BlockSpec(memory_space=pltpu.SMEM)
-PARAMS = pltpu.CompilerParams(vmem_limit_bytes=32 * 1024 * 1024)
-
-
-def call(kernel, in_specs, out_shape):
+MIB = 1024 * 1024
+
+
+def call(kernel, in_specs, out_shape, limit=32):
     out_specs = VMEM if not isinstance(out_shape, tuple) else (VMEM,) * len(out_shape)
     return pl.pallas_call(
-        kernel, in_specs=in_specs, out_specs=out_specs, out_shape=out_shape, compiler_params=PARAMS
+        kernel, in_specs=in_specs, out_specs=out_specs, out_shape=out_shape,
+        compiler_params=pltpu.CompilerParams(vmem_limit_bytes=limit * MIB),
     )
 
 
@@ -241,11 +258,12 @@
         return lax.all_to_all(array, "seq", 0, 0, axis_index_groups=members, tiled=True)
 
     received, beside = lax.optimization_barrier((exchange(state, within), beside))
-    same = jax.ShapeDtypeStruct(state.shape, F32)
+    received = received.reshape(inner, -1)
+    same = jax.ShapeDtypeStruct(received.shape, F32)
     sums, totals = call(
         functools.partial(inner_kernel, backward=backward),
         [SMEM, VMEM],
-        (same, jax.ShapeDtypeStruct((groups, state.shape[1]), F32)),
+        (same, jax.ShapeDtypeStruct((groups, received.shape[1]), F32)),
     )(beside[0], received)
     result = call(outer_kernel, [VMEM, VMEM], same)(sums, exchange(totals, across))
     return exchange(result, within), beside
@@ -260,7 +278,8 @@
     parts = split_blocks(lax.axis_size("seq"))[0]
     state_shape = jax.ShapeDtypeStruct((parts, (3 * size // parts + 1) * size), F32)
 
-    states = call(functools.partial(state_kernel, **sizes), [VMEM] * 2, state_shape)(keys, values)
+    states_shape = jax.ShapeDtypeStruct((parts, 1, state_shape.shape[1]), F32)
+    states = call(functools.partial(state_kernel, **sizes), [VMEM] * 2, states_shape, 60)(keys, values)
     d_out = lax.dot_general(
         lax.all_gather(out_grad, "head", axis=1, tiled=True),
         w_out,
@@ -269,14 +288,16 @@
     )
     group = (lax.axis_index("seq") // split_blocks(lax.axis_size("seq"))[0]).astype(jnp.int32)
     ridge_row = jnp.repeat(ridge, size)[None]
-    before, (group, d_out, ridge_row) = scan_over(
-        states, False, (group.reshape(1), d_out, ridge_row)
+    halved = jax.ShapeDtypeStruct((heads, 2 * size, 2 * size), BF16)
+    here = call(
+        functools.partial(local_kernel, **sizes), [VMEM] * 5, (local,) * 5 + (halved,) * 2
+    )(ridge_row, queries, keys, values, d_out)
+    before, (group, ridge_row, d_out, *here) = scan_over(
+        states, False, (group.reshape(1), ridge_row, d_out, *here)
     )
     grad_q, grad_k, grad_v, adjoints = call(
-        functools.partial(main_kernel, **sizes),
-        [VMEM] * 6,
-        (local, local, local, state_shape),
-    )(ridge_row, queries, keys, values, d_out, before)
+        functools.partial(main_kernel, **sizes), [VMEM] * 10, (local, local, local, state_shape)
+    )(ridge_row, d_out, *here, before)
     later, _ = scan_over(adjoints, True, (group,))
     grad_k, grad_v = call(
         functools.partial(final_kernel, **sizes), [VMEM] * 5, (local, local)

time: 140 us -> 138 us (0.986)
  local copies, waits for them, and re-layouts: 5.46 us -> 1.47 us
  Pallas kernels: 3.91 us -> 6.18 us
    unnamed x22 -> x18, local copies, waits for them, and re-layouts: 3.64 us -> 0.55 us
    pallas_call x2 -> x3, Pallas kernels: 2.35 us -> 4.62 us  [the longest x1 2.07 us: on_device(): call(functools.partial(state_kernel, **sizes), [VMEM] * 2, states_shape, 60)]
where the time goes in v3:
time: 138 us
  blocking collectives  108 us (78%)
  starting transfers between devices  19 us (14%)
  Pallas kernels  6.18 us (4%)
  waiting for transfers between devices  1.85 us (1%)
  local copies, waits for them, and re-layouts  1.47 us (1%)
    all_to_all x5, blocking collectives, exchange(): lax.all_to_all(array, 'seq', 0, 0, axis_index_groups=members, tiled=True)  94.7 us
    all_to_all x1, starting transfers between devices, exchange(): lax.all_to_all(array, 'seq', 0, 0, axis_index_groups=members, tiled=True)  19 us
    all_gather x1, blocking collectives, on_device(): lax.all_gather(out_grad, 'head', axis=1, tiled=True)  13.2 us
  transfers between devices with their start and end apart: 1, of which 1 were waited for; matrix products, arithmetic and copies ran while one was open for 0% of the time, Pallas kernels for 0%

profile of v3, /device:TPU:2, one launch (start us, length us, event | category | flops | bytes accessed | tf_op | source)
XLA Modules:
  0.0 137.6 jit_solution(10005531241365234717)
XLA Ops:
  0.6 0.0 copy-start
  0.6 2.1 %shard_map.85 = f32[16,1,3200]{2,1,0:T(1,128)} custom-call(f32[128,256]{1,0:T(8,128)} %k_ref.5, f32[128,256]{1,0:T(8,128)} %v_ref.5), custom_call_target="tpu_custom_call" | custom-call | tf_op jit(solution)/shard_map/pallas_call | solution.py:282
  2.7 0.0 copy-start.4
  2.7 19.0 %all-to-all-start = ((f32[16,1,3200]{2,1,0:T(1,128)}), f32[16,1,3200]{2,1,0:T(1,128)S(1)}, u32[]{:S(2)}, u32[]{:S(2)}) async-start(f32[16,1,3200]{2,1,0:T(1,128)} %shard_map.85), calls=%async_computation | async-start | bytes 409600 | tf_op jit(solution)/shard_map/all_to_all | solution.py:258
  21.7 0.0 copy-done.4
  21.7 13.2 %all_gather.3 = bf16[128,2048]{1,0:T(8,128)(2,1)S(1)} all-gather(bf16[128,256]{1,0:T(8,128)(2,1)S(1)} %copy-done.4), channel_id=1, replica_groups=mesh['seq'=128,'head'=8] {'head'}, dimensions={1}, use_global_device_ids=true | all-gather | bytes 589824 | tf_op jit(solution)/shard_map/all_gather | solution.py:284
  34.9 0.0 copy-done
  34.9 0.0 copy-start.5
  34.9 0.0 copy-start.1
  34.9 0.0 copy-start.2
  34.9 0.0 copy-start.3
  34.9 0.5 fusion.do_ref
  35.4 0.1 copy-done.5
  35.6 0.1 broadcast_in_dim.3
  35.6 0.2 copy-done.1
  35.8 0.1 copy-done.2
  35.9 0.1 copy-done.3
  36.0 0.6 shard_map.86
  36.5 1.9 %all-to-all-done = f32[16,1,3200]{2,1,0:T(1,128)S(1)} async-done(((f32[16,1,3200]{2,1,0:T(1,128)}), f32[16,1,3200]{2,1,0:T(1,128)S(1)}, u32[]{:S(2)}, u32[]{:S(2)}) %all-to-all-start) | async-done | bytes 204832 | tf_op jit(solution)/shard_map/all_to_all | solution.py:258
  38.4 0.2 shard_map.87
  38.6 0.1 copy.10
  38.7 15.7 %all_to_all.61 = f32[8,1,3200]{2,1,0:T(1,128)S(1)} all-to-all(f32[8,1,3200]{2,1,0:T(1,128)S(1)} %copy.10), channel_id=1, replica_groups={{0,128,256,384,512,640,768,896},{8,136,264,392,520,648,776,904},{16,144..., dimensions={0} | all-to-all | bytes 204800 | tf_op jit(solution)/shard_map/all_to_all | solution.py:258
  54.5 0.2 copy.11
  54.7 26.1 %all_to_all.62 = f32[16,1,3200]{2,1,0:T(1,128)S(1)} all-to-all(f32[16,1,3200]{2,1,0:T(1,128)S(1)} %copy.11), channel_id=1, replica_groups={{0,8,16,24,32,40,48,56,64,72,80,88,96,104,112,120},{128,136,144,152,160..., dimensions={0} | all-to-all | bytes 409600 | tf_op jit(solution)/shard_map/all_to_all | solution.py:258
  80.9 2.0 %shard_map.89 = (f32[128,256]{1,0:T(8,128)}, f32[128,256]{1,0:T(8,128)S(1)}, f32[128,256]{1,0:T(8,128)S(1)}, f32[16,3200]{1,0:T(8,128)S(1)}) custom-call(f32[1,256]{1,0:T(1,128)S(1)} %bitcast.39, f32[128,256]{1,0:T(8,128)S(1)} %fusion.do_ref, f32[128,256]{1,0:T(8,128)S(1)} %get-tuple-element.42.q_ref, f32[128,256]{1,0:T(8,128)S(1)} %get-tuple-element.43.s0_ref, ...), custom_call_target="tpu_custom_call" | custom-call | tf_op jit(solution)/shard_map/pallas_call | solution.py:298
  82.8 0.2 copy.12
  83.1 20.4 %all_to_all.63 = f32[16,1,3200]{2,1,0:T(1,128)S(1)} all-to-all(f32[16,1,3200]{2,1,0:T(1,128)S(1)} %copy.12), channel_id=1, replica_groups={{0,8,16,24,32,40,48,56,64,72,80,88,96,104,112,120},{128,136,144,152,160..., dimensions={0} | all-to-all | bytes 409600 | tf_op jit(solution)/shard_map/all_to_all | solution.py:258
  103.5 0.2 shard_map.90
  103.7 0.1 copy.13
  103.8 11.8 %all_to_all.64 = f32[8,1,3200]{2,1,0:T(1,128)S(1)} all-to-all(f32[8,1,3200]{2,1,0:T(1,128)S(1)} %copy.13), channel_id=1, replica_groups={{0,128,256,384,512,640,768,896},{8,136,264,392,520,648,776,904},{16,144..., dimensions={0} | all-to-all | bytes 204800 | tf_op jit(solution)/shard_map/all_to_all | solution.py:258
  115.7 0.2 copy.14
  115.9 20.7 %all_to_all.65 = f32[16,1,3200]{2,1,0:T(1,128)S(1)} all-to-all(f32[16,1,3200]{2,1,0:T(1,128)S(1)} %copy.14), channel_id=1, replica_groups={{0,8,16,24,32,40,48,56,64,72,80,88,96,104,112,120},{128,136,144,152,160..., dimensions={0} | all-to-all | bytes 409600 | tf_op jit(solution)/shard_map/all_to_all | solution.py:258
  136.6 1.0 shard_map.92
  (8 shorter events, 0.1 us)
Async XLA Ops:
  0.6 34.3 %copy-start = (bf16[256,2048]{1,0:T(8,128)(2,1)S(1)}, bf16[256,2048]{1,0:T(8,128)(2,1)}, u32[]{:S(2)}) copy-start(bf16[256,2048]{1,0:T(8,128)(2,1)} %param.10) | copy-start | bytes 3145732
  2.7 19.0 %copy-start.4 = (bf16[128,256]{1,0:T(8,128)(2,1)S(1)}, bf16[128,256]{1,0:T(8,128)(2,1)}, u32[]{:S(2)}) copy-start(bf16[128,256]{1,0:T(8,128)(2,1)} %param.9) | copy-start | bytes 196612
  2.7 35.7 %all-to-all-start = ((f32[16,1,3200]{2,1,0:T(1,128)}), f32[16,1,3200]{2,1,0:T(1,128)S(1)}, u32[]{:S(2)}, u32[]{:S(2)}) async-start(f32[16,1,3200]{2,1,0:T(1,128)} %shard_map.85), calls=%async_computation | async-start | bytes 409600 | tf_op jit(solution)/shard_map/all_to_all | solution.py:258
  34.9 0.7 copy-start.5
  34.9 0.9 copy-start.1
  34.9 1.0 copy-start.2
  34.9 1.0 copy-start.3

commit v4 on v3

--- a/solution.py
+++ b/solution.py
@@ -135,25 +135,30 @@
     return jnp.where(rows >= cols, scores, 0.0)
 
 
-def local_kernel(
-    ridge_ref, q_ref, k_ref, v_ref, do_ref,
-    q_out, s0_ref, a0_ref, sw_ref, xb_ref, plain_ref, turned_ref, *, heads, size,
+def query_kernel(
+    q_ref, k_ref, v_ref, q_out, s0_ref, a0_ref, plain_ref, turned_ref, values_ref, *, heads, size
 ):
     q_out[...] = q_ref[...]
     for h in range(heads):
         here = slice(h * size, (h + 1) * size)
         q, k = q_ref[:, here], k_ref[:, here]
         plain, turned = right(k), right_t(k)
-        plain_ref[h], turned_ref[h] = plain, turned
+        plain_ref[h], turned_ref[h], values_ref[h] = plain, turned, right_t(v_ref[:, here])
         s0 = causal(mul_t(left(q), turned))
-        sw = causal(mul_t(left(do_ref[:, here]), right_t(v_ref[:, here])))
-        s0_ref[:, here], sw_ref[:, here] = s0, sw
-        a0_ref[:, here] = mul(left(s0), plain) + ridge_ref[:, here] * q
-        xb_ref[:, here] = mul(left(sw), plain)
+        s0_ref[:, here] = s0
+        a0_ref[:, here] = mul(left(s0), plain)
+
+
+def cotangent_kernel(do_ref, plain_ref, values_ref, sw_ref, xb_ref, *, heads, size):
+    for h in range(heads):
+        here = slice(h * size, (h + 1) * size)
+        sw = causal(mul_t(left(do_ref[:, here]), values_ref[h]))
+        sw_ref[:, here] = sw
+        xb_ref[:, here] = mul(left(sw), plain_ref[h])
 
 
 def main_kernel(
-    ridge_ref, do_ref, q_ref, s0_ref, a0_ref, sw_ref, xb_ref, plain_ref, turned_ref, state_ref,
+    ridge_ref, do_ref, q_ref, s0_ref, a0_ref, plain_ref, turned_ref, sw_ref, xb_ref, state_ref,
     gq_ref, gk_ref, gv_ref, out_ref, *, heads, size,
 ):
     each = range(heads)
@@ -170,7 +175,9 @@
         image = [mul(left(scores[h]), plain_ref[h]) + carried[h] + ridge[h] * p[h] for h in each]
         return scores, image
 
-    a0 = [column_block(a0_ref, h, size) + mul(left(q[h]), cov[h]) for h in each]
+    a0 = [
+        column_block(a0_ref, h, size) + ridge[h] * q[h] + mul(left(q[h]), cov[h]) for h in each
+    ]
     xb = [column_block(xb_ref, h, size) + mul(left(do[h]), valkey[h]) for h in each]
 
     n0 = [row_dot(q[h], q[h]) for h in each]
@@ -221,7 +228,10 @@
     pack(cov_out, valkey_out, out_ref)
 
 
-def final_kernel(k_ref, v_ref, gk_ref, gv_ref, state_ref, gk_out, gv_out, *, heads, size):
+def final_kernel(
+    k_ref, v_ref, gq_ref, gk_ref, gv_ref, state_ref, gq_out, gk_out, gv_out, *, heads, size
+):
+    gq_out[...] = gq_ref[...]
     cov, valkey = unpack(state_ref, size)
     for h in range(heads):
         here = slice(h * size, (h + 1) * size)
@@ -289,9 +299,12 @@
     group = (lax.axis_index("seq") // split_blocks(lax.axis_size("seq"))[0]).astype(jnp.int32)
     ridge_row = jnp.repeat(ridge, size)[None]
     halved = jax.ShapeDtypeStruct((heads, 2 * size, 2 * size), BF16)
-    here = call(
-        functools.partial(local_kernel, **sizes), [VMEM] * 5, (local,) * 5 + (halved,) * 2
-    )(ridge_row, queries, keys, values, d_out)
+    *here, value_halves = call(
+        functools.partial(query_kernel, **sizes), [VMEM] * 3, (local,) * 3 + (halved,) * 3
+    )(queries, keys, values)
+    here += call(functools.partial(cotangent_kernel, **sizes), [VMEM] * 3, (local,) * 2)(
+        d_out, here[3], value_halves
+    )
     before, (group, ridge_row, d_out, *here) = scan_over(
         states, False, (group.reshape(1), ridge_row, d_out, *here)
     )
@@ -299,10 +312,9 @@
         functools.partial(main_kernel, **sizes), [VMEM] * 10, (local, local, local, state_shape)
     )(ridge_row, d_out, *here, before)
     later, _ = scan_over(adjoints, True, (group,))
-    grad_k, grad_v = call(
-        functools.partial(final_kernel, **sizes), [VMEM] * 5, (local, local)
-    )(keys, values, grad_k, grad_v, later)
-    return grad_q, grad_k, grad_v
+    return call(functools.partial(final_kernel, **sizes), [VMEM] * 6, (local,) * 3)(
+        keys, values, grad_q, grad_k, grad_v, later
+    )
 
 
 def solution(mesh):

time: 138 us -> 139 us (level)
  transfers between devices with their start and end apart: 1 -> 1, of which waited for: 1 -> 1; matrix products, arithmetic and copies ran while one was open for 0% -> 0% of each run, Pallas kernels for 0% -> 1%
where the time goes in v4:
time: 139 us; the launch traced here: 138 us
  blocking collectives  109 us (78%)
  starting transfers between devices  19 us (14%)
  Pallas kernels  6.36 us (5%)
  waiting for transfers between devices  1.58 us (1%)
    all_to_all x5, blocking collectives, exchange(): lax.all_to_all(array, 'seq', 0, 0, axis_index_groups=members, tiled=True)  95.6 us
    all_to_all x1, starting transfers between devices, exchange(): lax.all_to_all(array, 'seq', 0, 0, axis_index_groups=members, tiled=True)  19 us
    all_gather x1, blocking collectives, on_device(): lax.all_gather(out_grad, 'head', axis=1, tiled=True)  13.1 us
  transfers between devices with their start and end apart: 1, of which 1 were waited for; matrix products, arithmetic and copies ran while one was open for 0% of the time, Pallas kernels for 1%

profile of v4, /device:TPU:2, one launch (start us, length us, event | category | flops | bytes accessed | tf_op | source)
XLA Modules:
  0.0 138.3 jit_solution(6438347339397396753)
XLA Ops:
  0.6 0.0 copy-start
  0.6 2.1 %shard_map.85 = f32[16,1,3200]{2,1,0:T(1,128)} custom-call(f32[128,256]{1,0:T(8,128)} %k_ref.5, f32[128,256]{1,0:T(8,128)} %v_ref.5), custom_call_target="tpu_custom_call" | custom-call | tf_op jit(solution)/shard_map/pallas_call | solution.py:292
  2.7 0.0 copy-start.1
  2.7 0.0 copy-start.2
  2.7 0.0 copy-start.3
  2.7 19.0 %all-to-all-start = ((f32[16,1,3200]{2,1,0:T(1,128)}), f32[16,1,3200]{2,1,0:T(1,128)S(1)}, u32[]{:S(2)}, u32[]{:S(2)}) async-start(f32[16,1,3200]{2,1,0:T(1,128)} %shard_map.85), calls=%async_computation | async-start | bytes 409600 | tf_op jit(solution)/shard_map/all_to_all | solution.py:268
  21.7 0.0 copy-done.1
  21.7 0.0 copy-done.2
  21.8 0.0 copy-done.3
  21.8 0.0 copy-start.4
  21.8 0.5 shard_map.86
  22.3 0.3 copy-done.4
  22.6 13.1 %all_gather.3 = bf16[128,2048]{1,0:T(8,128)(2,1)S(1)} all-gather(bf16[128,256]{1,0:T(8,128)(2,1)S(1)} %copy-done.4), channel_id=1, replica_groups=mesh['seq'=128,'head'=8] {'head'}, dimensions={1}, use_global_device_ids=true | all-gather | bytes 589824 | tf_op jit(solution)/shard_map/all_gather | solution.py:294
  35.8 0.0 copy-done
  35.8 0.5 fusion.do_ref
  36.3 0.5 shard_map.87
  36.8 0.0 copy-start.5
  36.8 1.6 %all-to-all-done = f32[16,1,3200]{2,1,0:T(1,128)S(1)} async-done(((f32[16,1,3200]{2,1,0:T(1,128)}), f32[16,1,3200]{2,1,0:T(1,128)S(1)}, u32[]{:S(2)}, u32[]{:S(2)}) %all-to-all-start) | async-done | bytes 204832 | tf_op jit(solution)/shard_map/all_to_all | solution.py:268
  38.4 0.0 copy-done.5
  38.4 0.1 broadcast_in_dim.3
  38.5 0.2 shard_map.88
  38.7 0.1 copy.10
  38.8 15.7 %all_to_all.61 = f32[8,1,3200]{2,1,0:T(1,128)S(1)} all-to-all(f32[8,1,3200]{2,1,0:T(1,128)S(1)} %copy.10), channel_id=1, replica_groups={{0,128,256,384,512,640,768,896},{8,136,264,392,520,648,776,904},{16,144..., dimensions={0} | all-to-all | bytes 204800 | tf_op jit(solution)/shard_map/all_to_all | solution.py:268
  54.5 0.2 copy.11
  54.8 27.0 %all_to_all.62 = f32[16,1,3200]{2,1,0:T(1,128)S(1)} all-to-all(f32[16,1,3200]{2,1,0:T(1,128)S(1)} %copy.11), channel_id=1, replica_groups={{0,8,16,24,32,40,48,56,64,72,80,88,96,104,112,120},{128,136,144,152,160..., dimensions={0} | all-to-all | bytes 409600 | tf_op jit(solution)/shard_map/all_to_all | solution.py:268
  81.8 1.6 %shard_map.90 = (f32[128,256]{1,0:T(8,128)S(1)}, f32[128,256]{1,0:T(8,128)S(1)}, f32[128,256]{1,0:T(8,128)S(1)}, f32[16,3200]{1,0:T(8,128)S(1)}) custom-call(f32[1,256]{1,0:T(1,128)S(1)} %bitcast.38, f32[128,256]{1,0:T(8,128)S(1)} %fusion.do_ref, f32[128,256]{1,0:T(8,128)S(1)} %get-tuple-element.42.q_ref, f32[128,256]{1,0:T(8,128)S(1)} %get-tuple-element.43.s0_ref, ...), custom_call_target="tpu_custom_call" | custom-call | tf_op jit(solution)/shard_map/pallas_call | solution.py:311
  83.5 0.2 copy.12
  83.7 20.4 %all_to_all.63 = f32[16,1,3200]{2,1,0:T(1,128)S(1)} all-to-all(f32[16,1,3200]{2,1,0:T(1,128)S(1)} %copy.12), channel_id=1, replica_groups={{0,8,16,24,32,40,48,56,64,72,80,88,96,104,112,120},{128,136,144,152,160..., dimensions={0} | all-to-all | bytes 409600 | tf_op jit(solution)/shard_map/all_to_all | solution.py:268
  104.1 0.2 shard_map.91
  104.3 0.1 copy.13
  104.4 11.8 %all_to_all.64 = f32[8,1,3200]{2,1,0:T(1,128)S(1)} all-to-all(f32[8,1,3200]{2,1,0:T(1,128)S(1)} %copy.13), channel_id=1, replica_groups={{0,128,256,384,512,640,768,896},{8,136,264,392,520,648,776,904},{16,144..., dimensions={0} | all-to-all | bytes 204800 | tf_op jit(solution)/shard_map/all_to_all | solution.py:268
  116.3 0.2 copy.14
  116.5 20.7 %all_to_all.65 = f32[16,1,3200]{2,1,0:T(1,128)S(1)} all-to-all(f32[16,1,3200]{2,1,0:T(1,128)S(1)} %copy.14), channel_id=1, replica_groups={{0,8,16,24,32,40,48,56,64,72,80,88,96,104,112,120},{128,136,144,152,160..., dimensions={0} | all-to-all | bytes 409600 | tf_op jit(solution)/shard_map/all_to_all | solution.py:268
  137.2 1.1 shard_map.93
  (8 shorter events, 0.1 us)
Async XLA Ops:
  0.6 35.1 %copy-start = (bf16[256,2048]{1,0:T(8,128)(2,1)S(1)}, bf16[256,2048]{1,0:T(8,128)(2,1)}, u32[]{:S(2)}) copy-start(bf16[256,2048]{1,0:T(8,128)(2,1)} %param.10) | copy-start | bytes 3145732
  2.7 19.0 %copy-start.1 = (f32[128,256]{1,0:T(8,128)S(1)}, f32[128,256]{1,0:T(8,128)}, u32[]{:S(2)}) copy-start(f32[128,256]{1,0:T(8,128)} %k_ref.5) | copy-start | bytes 393220
  2.7 19.0 %copy-start.2 = (f32[128,256]{1,0:T(8,128)S(1)}, f32[128,256]{1,0:T(8,128)}, u32[]{:S(2)}) copy-start(f32[128,256]{1,0:T(8,128)} %v_ref.5) | copy-start | bytes 393220
  2.7 19.0 %copy-start.3 = (f32[128,256]{1,0:T(8,128)S(1)}, f32[128,256]{1,0:T(8,128)}, u32[]{:S(2)}) copy-start(f32[128,256]{1,0:T(8,128)} %q_ref.1) | copy-start | bytes 393220
  2.7 35.7 %all-to-all-start = ((f32[16,1,3200]{2,1,0:T(1,128)}), f32[16,1,3200]{2,1,0:T(1,128)S(1)}, u32[]{:S(2)}, u32[]{:S(2)}) async-start(f32[16,1,3200]{2,1,0:T(1,128)} %shard_map.85), calls=%async_computation | async-start | bytes 409600 | tf_op jit(solution)/shard_map/all_to_all | solution.py:268
  21.8 0.8 copy-start.4
  36.8 1.6 %copy-start.5 = (f32[2]{0:T(128)S(1)}, f32[2]{0:T(128)}, u32[]{:S(2)}) copy-start(f32[2]{0:T(128)} %param.11) | copy-start | bytes 28
